TPU v7x, 32 devices: a whole 2x2x4 slice. The times are simulated.
32 devices in a mesh: hist: 8 (over y, x, core), second: 4 (over z).
Axes of the slice: x: 2, y: 2, z: 4, core: 2. Of those that a mesh axis runs over, the one named last changes fastest.
Arguments:
- history: bfloat16 [8192, 8192], P('hist', 'second'), may hold values from -0.0625 to 0.0625
- self_rows: bfloat16 [256, 8192], P(None, 'hist'), may hold values from -6 to 6
- edge_rows: bfloat16 [128, 8192], P(None, 'second'), may hold values from -6 to 6
- step_inv: float32 [128, 128], replicated, may hold values from -0.08 to 0.98, as said below
- coupling: float32 [128], replicated, may hold values from 0.1 to 1
- reach: int32 [3, 64], replicated, may hold values from 1 to 64, as said below
Outputs:
- green_last: bfloat16 [256, 8192], P(None, 'second')
Inputs may be any that keep to these rules, and one draw needn't show every extreme that they name: `step_inv`: entries other than the diagonal lie within 0.08 of zero; diagonal entries between 0.5 and 0.9. reach[b, c] is at least c + 1 and at most min(64, c + 2 * b + 4).
All inputs are finite; a program needn't handle non-finite values.
Results may differ from a plain program's by a relative error of at most 0.014.
Values may be sent and summed in bfloat16 or wider, within the bound.
A program may use at most 64 MiB of HBM per device.

v0:
```python
import jax
import jax.numpy as jnp
from jax import lax
from jax.sharding import PartitionSpec as P


def screened(block_rows, weights):
    square = block_rows * block_rows
    return weights[:, None] * block_rows * square / (1.0 + square)


def advance(green_now, integral, step_inv, row_t, time_steps):
    rows_out = []
    for step_number in range(time_steps):
        source = green_now + integral[step_number * row_t : (step_number + 1) * row_t]
        green_now = jnp.dot(
            step_inv, source, precision=lax.Precision.HIGHEST, preferred_element_type=jnp.float32
        )
        rows_out.append(green_now)
    return (green_now, jnp.concatenate(rows_out, 0))


def local(history, self_rows, edge_rows, step_inv, coupling, reach):
    hist_count = lax.axis_size("hist")
    second_count = lax.axis_size("second")
    hist_place = lax.axis_index("hist")
    second_place = lax.axis_index("second")
    rows_loc, cols_loc = history.shape
    row_t = step_inv.shape[0]
    time_steps = self_rows.shape[0] // row_t
    past_loc = rows_loc // row_t
    tiles_loc = cols_loc // row_t
    ratio_axes = hist_count // second_count
    past_ids = hist_place * past_loc + jnp.arange(past_loc, dtype=jnp.int32)
    weights = jnp.tile(coupling, time_steps)
    tiled_hist = history.reshape(past_loc, row_t, tiles_loc, row_t)
    blocks = reach.shape[0]
    sigma_rows = self_rows
    green_now = edge_rows.astype(jnp.float32)
    finished = None
    for moment in range(blocks):
        limit_row = lax.dynamic_slice_in_dim(reach[moment], second_place * tiles_loc, tiles_loc)
        live_mask = past_ids[:, None] < limit_row[None, :]
        masked = jnp.where(
            live_mask[:, None, :, None], tiled_hist, jnp.zeros((), history.dtype)
        ).reshape(rows_loc, cols_loc)
        partial_value = jnp.dot(sigma_rows, masked, preferred_element_type=jnp.float32)
        final_block = moment + 1 == blocks
        fresh_rows = None
        integral = lax.psum(partial_value.astype(jnp.bfloat16), "hist").astype(jnp.float32)
        green_now, block_rows = advance(green_now, integral, step_inv, row_t, time_steps)
        if final_block:
            finished = block_rows.astype(jnp.bfloat16)
        else:
            fresh_rows = screened(block_rows, weights).astype(jnp.bfloat16)
        if not final_block:
            own_piece = lax.dynamic_slice_in_dim(
                fresh_rows, hist_place % ratio_axes * rows_loc, rows_loc, 1
            )
            holder = second_place == hist_place // ratio_axes
            kept_piece = jnp.where(
                holder, own_piece.astype(jnp.float32), jnp.zeros((), jnp.float32)
            )
            sigma_rows = lax.psum(kept_piece.astype(jnp.bfloat16), "second")
    return finished


def solution(mesh):
    placed = (P("hist", "second"), P(None, "hist"), P(None, "second"), P(), P(), P())
    return jax.shard_map(
        local, mesh=mesh, in_specs=placed, out_specs=P(None, "second"), check_vma=False
    )
```

profile of v0, /device:TPU:25, one launch (start us, length us, event | category | flops | bytes accessed | tf_op | source)
XLA Modules:
  0.0 292.0 jit_solution(8897772989769936309)
XLA Ops:
  6.5 0.8 fusion.20
  7.4 0.1 fusion.14
  7.5 0.1 broadcast_compare_fusion
  7.6 0.6 broadcast_in_dim.44
  8.2 5.1 %fusion.6 = bf16[256,2048]{0,1:T(8,128)(2,1)} fusion(bf16[256,1024]{1,0:T(8,128)(2,1)S(1)} %copy-done, bf16[1024,2048]{1,0:T(8,128)(2,1)} %param.6, pred[128,8,16,128]{3,2,1,0:T(8,128)(4,1)S(1)} %bitcast.56), kind=kOutput, calls=%fused_computation.9 | convolution fusion | flops 1076363264 | bytes 7864320 | tf_op jit(solution)/shard_map/dot_general | solution.py:47
  13.4 0.3 copy.7
  13.7 0.2 copy-done.5
  14.0 56.0 %all-reduce.6.cloned.1.call-done = bf16[256,2048]{0,1:T(8,128)(2,1)} async-done(((bf16[256,2048]{0,1:T(8,128)(2,1)}), bf16[256,2048]{0,1:T(8,128)(2,1)}) %all-reduce.6.cloned.1.call-update) | async-done | bytes 1048592 | tf_op jit(solution)/shard_map/psum | solution.py:50
  70.0 1.4 convert_element_type.46
  71.4 1.0 convolution_bitcast_fusion.4
  72.4 1.0 convolution_bitcast_fusion.3
  73.4 1.1 select_convert_fusion.1
  74.5 36.1 %all-reduce.8.cloned.1.call-done = bf16[256,1024]{0,1:T(8,128)(2,1)} async-done(((bf16[256,1024]{0,1:T(8,128)(2,1)}), bf16[256,1024]{0,1:T(8,128)(2,1)}) %all-reduce.8.cloned.1.call-update) | async-done | bytes 524304 | tf_op jit(solution)/shard_map/psum | solution.py:64
  110.7 0.6 broadcast_in_dim.48
  111.3 0.4 copy-done.4
  111.7 5.5 %fusion.4 = bf16[256,2048]{0,1:T(8,128)(2,1)} fusion(bf16[256,1024]{0,1:T(8,128)(2,1)S(1)} %copy-done.4, bf16[1024,2048]{1,0:T(8,128)(2,1)} %param.6, pred[128,8,16,128]{3,2,1,0:T(8,128)(4,1)S(1)} %bitcast.54), kind=kOutput, calls=%fused_computation.7 | convolution fusion | flops 1076363264 | bytes 7864320 | tf_op jit(solution)/shard_map/dot_general | solution.py:47
  117.3 58.0 %all-reduce.10.cloned.1.call-done = bf16[256,2048]{0,1:T(8,128)(2,1)} async-done(((bf16[256,2048]{0,1:T(8,128)(2,1)}), bf16[256,2048]{0,1:T(8,128)(2,1)}) %all-reduce.10.cloned.1.call-update) | async-done | bytes 1048592 | tf_op jit(solution)/shard_map/psum | solution.py:50
  175.3 1.4 convert_element_type.51
  176.7 1.0 convolution_bitcast_fusion.2
  177.7 1.0 convolution_bitcast_fusion.1
  178.7 1.1 select_convert_fusion
  179.8 0.2 all-reduce.14.cloned.1.call-start
  180.0 36.0 %all-reduce.12.cloned.1.call-done = bf16[256,1024]{0,1:T(8,128)(2,1)} async-done(((bf16[256,1024]{0,1:T(8,128)(2,1)}), bf16[256,1024]{0,1:T(8,128)(2,1)}) %all-reduce.12.cloned.1.call-update) | async-done | bytes 524304 | tf_op jit(solution)/shard_map/psum | solution.py:64
  215.9 0.6 broadcast_in_dim.50
  216.6 0.4 copy-done.3
  217.0 5.5 %fusion.3 = bf16[256,2048]{0,1:T(8,128)(2,1)} fusion(bf16[256,1024]{0,1:T(8,128)(2,1)S(1)} %copy-done.3, bf16[1024,2048]{1,0:T(8,128)(2,1)} %param.6, pred[128,8,16,128]{3,2,1,0:T(8,128)(4,1)S(1)} %bitcast.55), kind=kOutput, calls=%fused_computation.6 | convolution fusion | flops 1076363264 | bytes 7864320 | tf_op jit(solution)/shard_map/dot_general | solution.py:47
  222.5 58.1 %all-reduce.14.cloned.1.call-done = bf16[256,2048]{0,1:T(8,128)(2,1)} async-done(((bf16[256,2048]{0,1:T(8,128)(2,1)}), bf16[256,2048]{0,1:T(8,128)(2,1)}) %all-reduce.14.cloned.1.call-update) | async-done | bytes 1048592 | tf_op jit(solution)/shard_map/psum | solution.py:50
  280.6 1.4 convert_element_type.56
  282.0 1.0 fusion.21
  283.0 1.0 fusion.7
  283.9 0.1 pad_maximum_fusion
  284.1 1.4 copy.16
  (21 shorter events, 0.3 us)
Async XLA Ops:
  6.5 1.6 copy-start
  6.5 63.5 %all-reduce.6.cloned.1.call-start = ((), (), s32[]{:S(2)}) async-start(), calls=%async_computation | async-start | bytes 2097152 | tf_op jit(solution)/shard_map/psum | solution.py:50
  8.2 5.2 %copy-start.2 = (bf16[128,2048]{1,0:T(8,128)(2,1)S(1)}, bf16[128,2048]{1,0:T(8,128)(2,1)}, u32[]{:S(2)}) copy-start(bf16[128,2048]{1,0:T(8,128)(2,1)} %param.8) | copy-start | bytes 1572868
  13.3 0.7 copy-start.5
  13.4 97.3 %all-reduce.8.cloned.1.call-start = ((), (), s32[]{:S(2)}) async-start(), calls=%async_computation.1 | async-start | bytes 1048576 | tf_op jit(solution)/shard_map/psum | solution.py:64
  13.4 58.0 %copy-start.1 = (f32[128,128]{1,0:T(8,128)S(1)}, f32[128,128]{1,0:T(8,128)}, u32[]{:S(2)}) copy-start(f32[128,128]{1,0:T(8,128)} %param.9) | copy-start | bytes 196612
  74.5 100.8 %all-reduce.10.cloned.1.call-start = ((), (), s32[]{:S(2)}) async-start(), calls=%async_computation.2 | async-start | bytes 2097152 | tf_op jit(solution)/shard_map/psum | solution.py:50
  110.7 1.0 copy-start.4
  117.2 98.7 %all-reduce.12.cloned.1.call-start = ((), (), s32[]{:S(2)}) async-start(), calls=%async_computation.3 | async-start | bytes 1048576 | tf_op jit(solution)/shard_map/psum | solution.py:64
  179.8 100.8 %all-reduce.14.cloned.1.call-start = ((), (), s32[]{:S(2)}) async-start(), calls=%async_computation.4 | async-start | bytes 2097152 | tf_op jit(solution)/shard_map/psum | solution.py:50
  215.9 1.0 copy-start.3
Sparse Core Ops, SparseCore 0:
  13.5 56.5 all-reduce.5
  74.6 35.9 all-reduce.7
  117.3 57.9 all-reduce.9
  179.9 36.0 all-reduce.11
  222.6 57.9 all-reduce.13
where the time goes:
time: 295 us; the launch traced here: 292 us
  waiting for transfers between devices  244 us (83%)
  matrix products  22 us (7%)
  between operations  13.3 us (5%)
  other arithmetic  6.45 us (2%)
  local copies, waits for them, and re-layouts  5.57 us (2%)
    psum x3, waiting for transfers between devices, local(): lax.psum(partial_value.astype(jnp.bfloat16), 'hist').astype(jnp.float32)  172 us
    psum x2, waiting for transfers between devices, local(): sigma_rows = lax.psum(kept_piece.astype(jnp.bfloat16), 'second')  72.1 us
    dot_general x3, matrix products, local(): jnp.dot(sigma_rows, masked, preferred_element_type=jnp.float32)  16.1 us
    dot_general x6, matrix products, advance(): jnp.dot(step_inv, source, precision=lax.Precision.HIGHEST, preferred_elem...  5.91 us
  transfers between devices with their start and end apart: 5, of which 5 were waited for; matrix products, arithmetic and copies ran while one was open for 0% of the time, Pallas kernels for 0%

commit v1 on v0

v1 whole, which is shorter than its diff:
```python
import functools

import jax
import jax.numpy as jnp
from jax import lax
from jax.experimental import pallas as pl
from jax.experimental.pallas import tpu as pltpu
from jax.sharding import PartitionSpec as P

MESH = pl.DeviceIdType.MESH
CORES = 2
LANES = 128
BF16 = jnp.bfloat16
F32 = jnp.float32


def kernel(dims, hist_ref, self_ref, edge_ref, inv_ref, coup_ref, reach_ref, out_ref,
           masked, psend, pown, arecv, presum, rrecv, acc, green, weights, piece, relay, sig,
           a0_s, a0_r, a1_s, a1_r, z_s, z_r, home_s, fwd_s, sig_r, ag_s, ag_r, mg_s, mg_r):
    chips, planes, owners, width, row_t, steps, blocks = dims
    slab, cols = hist_ref.shape
    half = cols // CORES
    past, tiles = slab // row_t, cols // row_t
    h = lax.axis_index("hist")
    s = lax.axis_index("second")
    q, c = h // CORES, lax.rem(h, CORES)
    mate = q * CORES + 1 - c
    pending = []

    def when(cond, fn):
        if cond is True:
            fn()
        else:
            pl.when(cond)(fn)

    def both(*conds):
        total = True
        for cond in conds:
            if cond is True:
                continue
            total = cond if total is True else jnp.logical_and(total, cond)
        return total

    def owns(chip):
        return True if owners == chips else chip < owners

    def live(hh, plane):
        return hh * past < (plane + 1) * tiles - 1 + 2 * (blocks - 1) + 4

    def remote(src, dst, send, recv, hist_to, second_to):
        return pltpu.make_async_remote_copy(
            src_ref=src, dst_ref=dst, send_sem=send, recv_sem=recv,
            device_id={"hist": hist_to, "second": second_to}, device_id_type=MESH)

    def start(cond, copy):
        when(cond, copy.start)
        pending.append((cond, copy))

    live_me, live_mate = live(h, s), live(mate, s)
    mine = owns(q)

    barrier = pltpu.get_barrier_semaphore()

    def greet(hist_to, second_to):
        pl.semaphore_signal(barrier, inc=1, device_id={"hist": hist_to, "second": second_to},
                            device_id_type=MESH)

    greet(mate, s)
    for d in range(1, chips):
        greet(lax.rem(q + d, chips) * CORES + c, s)
    for d in range(1, planes):
        greet(h, lax.rem(s + d, planes))

    def chip_cols(chip):
        return pl.ds(pl.multiple_of(chip * width, width), width)

    def own_cols(chip, core):
        return pl.ds(pl.multiple_of(core * half + chip * width, width), width)

    def make_mask(b):
        def work():
            def body(ct, carry):
                limit = reach_ref[b, s * tiles + ct]
                at = pl.ds(pl.multiple_of(ct * row_t, row_t), row_t)
                for kt in range(past):
                    keep = jnp.where(h * past + kt < limit, 1.0, 0.0).astype(F32)
                    rows = slice(kt * row_t, (kt + 1) * row_t)
                    masked[b, rows, at] = hist_ref[rows, at] * jnp.full((row_t, row_t), keep, F32).astype(BF16)
                return carry
            lax.fori_loop(0, tiles, body, 0)
        when(live_me, work)

    def product(b, i, dst, core):
        idx = b * steps + i
        chunk = 256

        def body(t, carry):
            left = self_ref[i * row_t:(i + 1) * row_t, :] if b == 0 else sig[idx - steps]
            at = pl.ds(pl.multiple_of(core * half + t * chunk, chunk), chunk)
            to = pl.ds(pl.multiple_of(t * chunk, chunk), chunk)
            dst[idx, :, to] = jnp.dot(left, masked[b, :, at], preferred_element_type=F32).astype(BF16)
            return carry
        lax.fori_loop(0, half // chunk, body, 0)

    def a0_copy(idx):
        return remote(psend.at[idx], arecv.at[idx], a0_s.at[idx], a0_r.at[idx], mate, s)

    def sig_wait(idx):
        for e in range(1, chips):
            p = lax.rem(q + e, chips)

            def wait(p=p):
                spot = sig.at[idx, :, chip_cols(p)]
                remote(spot, spot, home_s.at[idx], sig_r.at[idx, p], p * CORES + c, s).wait_recv()
            when(owns(p), wait)

    def stage_product(b, i):
        idx = b * steps + i

        def first():
            if b:
                sig_wait(idx - steps)
            product(b, i, psend, 1 - c)
        when(live_me, first)
        if idx == 0:
            pl.semaphore_wait(barrier, 1 + (chips - 1) + (planes - 1))
        start(live_me, a0_copy(idx))
        when(live_me, lambda: product(b, i, pown, c))

    def a1_copy(idx, d):
        to = lax.rem(q + d, chips)
        return remote(presum.at[idx, :, chip_cols(to)], rrecv.at[idx, d - 1],
                      a1_s.at[idx, d - 1], a1_r.at[idx, d - 1], to * CORES + c, s)

    def stage_pair(b, i):
        idx = b * steps + i

        def pair():
            a0_copy(idx).wait_recv()
            presum[idx] = (pown[idx].astype(F32) + arecv[idx].astype(F32)).astype(BF16)

        def alone():
            presum[idx] = pown[idx]

        def other():
            a0_copy(idx).wait_recv()
            presum[idx] = arecv[idx]
        no_me, no_mate = jnp.logical_not(live_me), jnp.logical_not(live_mate)
        when(both(live_me, live_mate), pair)
        when(both(live_me, no_mate), alone)
        when(both(no_me, live_mate), other)
        for d in range(1, chips):
            to = lax.rem(q + d, chips)
            start(both(live(q * CORES, s), owns(to)), a1_copy(idx, d))

    def stage_reduce(b, i):
        idx = b * steps + i
        last = b + 1 == blocks

        def init():
            acc[...] = jnp.zeros_like(acc)

        def own():
            acc[...] = presum[idx, :, chip_cols(q)].astype(F32)

        when(mine, init)
        when(both(mine, live(q * CORES, s)), own)
        for d in range(1, chips):
            src = lax.rem(q + chips - d, chips)

            def add(d=d):
                a1_copy(idx, d).wait_recv()
                acc[...] += rrecv[idx, d - 1].astype(F32)
            when(both(mine, live(src * CORES, s)), add)

        def step():
            fresh = jnp.dot(inv_ref[...], green[...] + acc[...], precision=lax.Precision.HIGHEST,
                            preferred_element_type=F32)
            green[...] = fresh
            if last:
                out_ref[i * row_t:(i + 1) * row_t, own_cols(q, c)] = fresh.astype(BF16)
            else:
                square = fresh * fresh
                piece[idx] = (weights[...] * fresh * square / (1.0 + square)).astype(BF16)
        when(mine, step)
        if last:
            rows = slice(i * row_t, (i + 1) * row_t)
            spot = out_ref.at[rows, own_cols(q, c)]
            for d in range(1, chips):
                start(mine, remote(spot, spot, ag_s.at[i, d - 1], ag_r.at[i, d - 1],
                                   lax.rem(q + d, chips) * CORES + c, s))
            start(mine, remote(spot, spot, mg_s.at[i, 0], mg_r.at[i, 0], mate, s))
            return
        for d in range(planes - 1, 0, -1):
            to = lax.rem(s + d, planes)
            start(both(mine, live(s * CORES + c, to)),
                  remote(piece.at[idx], relay.at[idx, d - 1], z_s.at[idx, d - 1], z_r.at[idx, d - 1], h, to))
        spot = sig.at[idx, :, chip_cols(q)]
        start(both(mine, q != s), remote(piece.at[idx], spot, home_s.at[idx], sig_r.at[idx, q], s * CORES + c, s))

        def keep():
            sig[idx, :, chip_cols(q)] = piece[idx]
        when(both(mine, q == s), keep)

    def stage_forward(b, i):
        idx = b * steps + i
        for d in range(1, planes):
            src = lax.rem(s + planes - d, planes)
            used = both(mine, live(src * CORES + c, s))
            landed = relay.at[idx, d - 1]

            def wait(landed=landed, src=src, d=d):
                remote(landed, landed, z_s.at[idx, d - 1], z_r.at[idx, d - 1], h, src).wait_recv()
            when(used, wait)
            start(both(used, q != src),
                  remote(landed, sig.at[idx, :, chip_cols(q)], fwd_s.at[idx, d - 1], sig_r.at[idx, q],
                         src * CORES + c, s))

            def keep(d=d):
                sig[idx, :, chip_cols(q)] = relay[idx, d - 1]
            when(both(used, q == src), keep)

    def stage_gather(i):
        rows = slice(i * row_t, (i + 1) * row_t)
        for d in range(1, chips):
            src = lax.rem(q + chips - d, chips)
            spot = out_ref.at[rows, own_cols(src, c)]

            def wait(spot=spot, src=src, d=d):
                remote(spot, spot, ag_s.at[i, d - 1], ag_r.at[i, d - 1], src * CORES + c, s).wait_recv()
            when(owns(src), wait)
            start(owns(src), remote(spot, spot, mg_s.at[i, d], mg_r.at[i, d], mate, s))

    def stage_close(i):
        rows = slice(i * row_t, (i + 1) * row_t)
        for d in range(chips):
            src = lax.rem(q + chips - d, chips)

            def wait(src=src, d=d):
                spot = out_ref.at[rows, own_cols(src, 1 - c)]
                remote(spot, spot, mg_s.at[i, d], mg_r.at[i, d], mate, s).wait_recv()
            when(owns(src), wait)

    make_mask(0)
    for b in range(blocks):
        for i in range(steps):
            stage_product(b, i)
        for i in range(steps):
            stage_pair(b, i)
        if b == 0:
            row = lax.broadcasted_iota(jnp.int32, (row_t, row_t), 0)
            col = lax.broadcasted_iota(jnp.int32, (row_t, row_t), 1)
            spread = jnp.where(row == col, jnp.broadcast_to(coup_ref[...], (row_t, row_t)), 0.0)
            weights[...] = jnp.broadcast_to(jnp.sum(spread, axis=1, keepdims=True), weights.shape)

            def first_green():
                green[...] = edge_ref[:, own_cols(q, c)].astype(F32)
            when(mine, first_green)
        if b + 1 < blocks:
            make_mask(b + 1)
        for i in range(steps):
            stage_reduce(b, i)
        for i in range(steps):
            if b + 1 < blocks:
                stage_forward(b, i)
            else:
                stage_gather(i)
    for i in range(steps):
        stage_close(i)
    for cond, copy in pending:
        when(cond, copy.wait_send)


def local(hist_count, second_count, history, self_rows, edge_rows, step_inv, coupling, reach):
    slab, cols = history.shape
    row_t = step_inv.shape[0]
    steps = self_rows.shape[0] // row_t
    blocks = reach.shape[0]
    chips, planes = hist_count // CORES, second_count
    half = cols // CORES
    owners = min(chips, half // LANES)
    width = half // owners
    assert chips == planes and half == slab
    dims = (chips, planes, owners, width, row_t, steps, blocks)
    n, m = blocks * steps, (blocks - 1) * steps
    vmem = pl.BlockSpec(memory_space=pltpu.VMEM)
    dma = pltpu.SemaphoreType.DMA
    return pl.pallas_call(
        functools.partial(kernel, dims),
        out_shape=jax.ShapeDtypeStruct((steps * row_t, cols), BF16),
        in_specs=[vmem] * 5 + [pl.BlockSpec(memory_space=pltpu.SMEM)],
        out_specs=vmem,
        scratch_shapes=[
            pltpu.VMEM((blocks, slab, cols), BF16),
            pltpu.VMEM((n, row_t, half), BF16),
            pltpu.VMEM((n, row_t, half), BF16),
            pltpu.VMEM((n, row_t, half), BF16),
            pltpu.VMEM((n, row_t, half), BF16),
            pltpu.VMEM((n, chips - 1, row_t, width), BF16),
            pltpu.VMEM((row_t, width), F32),
            pltpu.VMEM((row_t, width), F32),
            pltpu.VMEM((row_t, width), F32),
            pltpu.VMEM((m, row_t, width), BF16),
            pltpu.VMEM((m, planes - 1, row_t, width), BF16),
            pltpu.VMEM((m, row_t, slab), BF16),
            dma((n,)), dma((n,)),
            dma((n, chips - 1)), dma((n, chips - 1)),
            dma((m, planes - 1)), dma((m, planes - 1)),
            dma((m,)), dma((m, planes - 1)), dma((m, chips)),
            dma((steps, chips - 1)), dma((steps, chips - 1)),
            dma((steps, chips)), dma((steps, chips)),
        ],
        compiler_params=pltpu.CompilerParams(
            collective_id=0, has_side_effects=True, vmem_limit_bytes=48 * 1024 * 1024),
        cost_estimate=pl.CostEstimate(
            flops=2 * blocks * steps * row_t * slab * cols, bytes_accessed=2 * slab * cols, transcendentals=0),
    )(history, self_rows, edge_rows, step_inv, coupling.reshape(1, row_t), reach)


def solution(mesh):
    placed = (P("hist", "second"), P(None, "hist"), P(None, "second"), P(), P(), P())
    return jax.shard_map(
        functools.partial(local, mesh.shape["hist"], mesh.shape["second"]),
        mesh=mesh, in_specs=placed, out_specs=P(None, "second"), check_vma=False
    )
```

time: 295 us -> 72.2 us (0.24)
  waiting for transfers between devices: 244 us -> 0 us
  Pallas kernels: 0 us -> 66.6 us
  matrix products: 22 us -> 0 us
  between operations: 13.3 us -> 0.01 us
  other arithmetic: 6.45 us -> 0 us
    psum x5 -> x0, waiting for transfers between devices: 244 us -> none  [the longest x3 172 us: local(): lax.psum(partial_value.astype(jnp.bfloat16), 'hist').astype(jnp.float32)]
    pallas_call x0 -> x1, Pallas kernels: none -> 66.6 us  [local(): pl.pallas_call(functools.partial(kernel, dims), out_shape=jax.ShapeDtypeS...]
    dot_general x9 -> x0, matrix products: 22 us -> none  [the longest x3 16.1 us: local(): jnp.dot(sigma_rows, masked, preferred_element_type=jnp.float32)]
    convert_element_type x5 -> x0, other arithmetic: 6.26 us -> none  [the longest x3 4.14 us: local(): lax.psum(partial_value.astype(jnp.bfloat16), 'hist').astype(jnp.float32)]
    unnamed x13 -> x11, local copies, waits for them, and re-layouts: 1.38 us -> 5.23 us
  transfers between devices with their start and end apart: 5 -> 0, of which waited for: 5 -> 0; matrix products, arithmetic and copies ran while one was open for 0% -> 0% of each run, Pallas kernels for 0% -> 0%
where the time goes in v1:
time: 72.2 us; the launch traced here: 71.9 us
  Pallas kernels  66.6 us (92%)
  local copies, waits for them, and re-layouts  5.23 us (7%)
    pallas_call x1, Pallas kernels, local(): pl.pallas_call(functools.partial(kernel, dims), out_shape=jax.ShapeDtypeS...  66.6 us
    unnamed x11, local copies, waits for them, and re-layouts  5.23 us

profile of v1, /device:TPU:25, one launch (start us, length us, event | category | flops | bytes accessed | tf_op | source)
XLA Modules:
  0.0 71.9 jit_solution(2327461044883110748)
XLA Ops:
  0.0 0.0 copy-start
  0.0 1.0 %copy-done = bf16[256,1024]{1,0:T(8,128)(2,1)S(1)} copy-done((bf16[256,1024]{1,0:T(8,128)(2,1)S(1)}, bf16[256,1024]{1,0:T(8,128)(2,1)}, u32[]{:S(2)}) %copy-start) | copy-done | bytes 524312
  1.0 0.0 copy-start.1
  1.0 1.0 %copy-done.1 = bf16[128,2048]{1,0:T(8,128)(2,1)S(1)} copy-done((bf16[128,2048]{1,0:T(8,128)(2,1)S(1)}, bf16[128,2048]{1,0:T(8,128)(2,1)}, u32[]{:S(2)}) %copy-start.1) | copy-done | bytes 524312
  2.1 0.0 copy-start.2
  2.1 0.8 %copy-done.2 = f32[128,128]{1,0:T(8,128)S(1)} copy-done((f32[128,128]{1,0:T(8,128)S(1)}, f32[128,128]{1,0:T(8,128)}, u32[]{:S(2)}) %copy-start.2) | copy-done | bytes 65560
  2.9 0.0 copy-start.3
  2.9 0.7 copy-done.3
  3.6 0.0 copy-start.4
  3.6 0.7 copy-done.4
  4.3 66.6 %shard_map.64 = bf16[256,2048]{1,0:T(8,128)(2,1)S(1)} custom-call(bf16[1024,2048]{1,0:T(8,128)(2,1)} %hist_ref.1, bf16[256,1024]{1,0:T(8,128)(2,1)S(1)} %copy-done, bf16[128,2048]{1,0:T(8,128)(2,1)S(1)} %copy-done.1, f32[128,128]{1,0:T(8,128)S(1)} %copy-done.2, f32[1,128]{1,0:T(1,128)S(1)} %bitcast.1, s32[3,64]{1,0:T(4,128)S(1)} %copy-done.3), custom_call_target="tpu_custom_call" | custom-call | flops 3221225472 | bytes 4194304 | tf_op jit(solution)/shard_map/pallas_call | solution.py:288
  70.9 1.0 %copy.8 = bf16[256,2048]{1,0:T(8,128)(2,1)} copy(bf16[256,2048]{1,0:T(8,128)(2,1)S(1)} %shard_map.64) | data formatting | bytes 2097152
Async XLA Ops:
  0.0 1.0 %copy-start = (bf16[256,1024]{1,0:T(8,128)(2,1)S(1)}, bf16[256,1024]{1,0:T(8,128)(2,1)}, u32[]{:S(2)}) copy-start(bf16[256,1024]{1,0:T(8,128)(2,1)} %self_ref.1) | copy-start | bytes 1572868
  1.0 1.0 %copy-start.1 = (bf16[128,2048]{1,0:T(8,128)(2,1)S(1)}, bf16[128,2048]{1,0:T(8,128)(2,1)}, u32[]{:S(2)}) copy-start(bf16[128,2048]{1,0:T(8,128)(2,1)} %edge_ref.1) | copy-start | bytes 1572868
  2.1 0.8 %copy-start.2 = (f32[128,128]{1,0:T(8,128)S(1)}, f32[128,128]{1,0:T(8,128)}, u32[]{:S(2)}) copy-start(f32[128,128]{1,0:T(8,128)} %inv_ref.1) | copy-start | bytes 196612
  2.9 0.7 copy-start.3
  3.6 0.7 copy-start.4

commit v2 on v1

--- a/solution.py
+++ b/solution.py
@@ -14,11 +14,11 @@
 F32 = jnp.float32
 
 
-def kernel(dims, hist_ref, self_ref, edge_ref, inv_ref, coup_ref, reach_ref, out_ref,
-           masked, psend, pown, arecv, presum, rrecv, acc, green, weights, piece, relay, sig,
+def kernel(dims, hist_hbm, self_hbm, edge_hbm, inv_hbm, coup_hbm, reach_ref, out_ref,
+           hist_ref, self_ref, edge_ref, inv_ref, coup_ref, load_s, masked, psend, pown, arecv, presum, rrecv, acc, green, weights, piece, relay, sig,
            a0_s, a0_r, a1_s, a1_r, z_s, z_r, home_s, fwd_s, sig_r, ag_s, ag_r, mg_s, mg_r):
-    chips, planes, owners, width, row_t, steps, blocks = dims
-    slab, cols = hist_ref.shape
+    chips, planes, owners, width, row_t, steps, blocks, below = dims
+    slab, cols = hist_hbm.shape
     half = cols // CORES
     past, tiles = slab // row_t, cols // row_t
     h = lax.axis_index("hist")
@@ -59,6 +59,21 @@
     live_me, live_mate = live(h, s), live(mate, s)
     mine = owns(q)
 
+    def half_load(core, n):
+        at = pl.ds(pl.multiple_of(core * half, half), half)
+        return pltpu.make_async_copy(hist_hbm.at[:, at], hist_ref.at[:, at], load_s.at[n])
+
+    load_first, load_second = half_load(1 - c, 0), half_load(c, 1)
+    load_self = pltpu.make_async_copy(self_hbm, self_ref, load_s.at[2])
+    edge_at = pl.ds(pl.multiple_of(c * half, half), half)
+    load_small = [
+        pltpu.make_async_copy(edge_hbm.at[:, edge_at], edge_ref, load_s.at[3]),
+        pltpu.make_async_copy(inv_hbm, inv_ref, load_s.at[4]),
+        pltpu.make_async_copy(coup_hbm, coup_ref, load_s.at[5]),
+    ]
+    for load in [load_first, load_self, load_second] + load_small:
+        load.start()
+
     barrier = pltpu.get_barrier_semaphore()
 
     def greet(hist_to, second_to):
@@ -77,17 +92,18 @@
     def own_cols(chip, core):
         return pl.ds(pl.multiple_of(core * half + chip * width, width), width)
 
-    def make_mask(b):
+    def make_mask(b, core):
         def work():
             def body(ct, carry):
-                limit = reach_ref[b, s * tiles + ct]
-                at = pl.ds(pl.multiple_of(ct * row_t, row_t), row_t)
+                tile = core * (tiles // CORES) + ct
+                limit = reach_ref[b, s * tiles + tile]
+                at = pl.ds(pl.multiple_of(tile * row_t, row_t), row_t)
                 for kt in range(past):
                     keep = jnp.where(h * past + kt < limit, 1.0, 0.0).astype(F32)
                     rows = slice(kt * row_t, (kt + 1) * row_t)
                     masked[b, rows, at] = hist_ref[rows, at] * jnp.full((row_t, row_t), keep, F32).astype(BF16)
                 return carry
-            lax.fori_loop(0, tiles, body, 0)
+            lax.fori_loop(0, tiles // CORES, body, 0)
         when(live_me, work)
 
     def product(b, i, dst, core):
@@ -191,10 +207,9 @@
                                    lax.rem(q + d, chips) * CORES + c, s))
             start(mine, remote(spot, spot, mg_s.at[i, 0], mg_r.at[i, 0], mate, s))
             return
-        for d in range(planes - 1, 0, -1):
-            to = lax.rem(s + d, planes)
-            start(both(mine, live(s * CORES + c, to)),
-                  remote(piece.at[idx], relay.at[idx, d - 1], z_s.at[idx, d - 1], z_r.at[idx, d - 1], h, to))
+        start(both(mine, s + 1 < planes), up_copy(idx, 0))
+        for e in range(1, below + 1):
+            start(both(mine, s >= e, live(s * CORES + c, s - e)), down_copy(idx, e, s - e))
         spot = sig.at[idx, :, chip_cols(q)]
         start(both(mine, q != s), remote(piece.at[idx], spot, home_s.at[idx], sig_r.at[idx, q], s * CORES + c, s))
 
@@ -202,23 +217,50 @@
             sig[idx, :, chip_cols(q)] = piece[idx]
         when(both(mine, q == s), keep)
 
-    def stage_forward(b, i):
-        idx = b * steps + i
-        for d in range(1, planes):
-            src = lax.rem(s + planes - d, planes)
-            used = both(mine, live(src * CORES + c, s))
+    def up_copy(idx, d):
+        src = piece.at[idx] if d == 0 else relay.at[idx, d - 1]
+        return remote(src, relay.at[idx, d], z_s.at[idx, d], z_r.at[idx, d], h, lax.rem(s + 1, planes))
+
+    def down_copy(idx, e, to):
+        slot = planes - 2 + e
+        return remote(piece.at[idx], relay.at[idx, slot], z_s.at[idx, slot], z_r.at[idx, slot],
+                      h, lax.rem(to + planes, planes))
+
+    def pass_on(idx, slot, src, used):
+        start(both(used, q != src),
+              remote(relay.at[idx, slot], sig.at[idx, :, chip_cols(q)], fwd_s.at[idx, slot], sig_r.at[idx, q],
+                     lax.rem(src + planes, planes) * CORES + c, s))
+
+        def keep():
+            sig[idx, :, chip_cols(q)] = relay[idx, slot]
+        when(both(used, q == src), keep)
+
+    def stage_up(b, i, d):
+        idx = b * steps + i
+        used = both(mine, s >= d)
+
+        def wait():
             landed = relay.at[idx, d - 1]
-
-            def wait(landed=landed, src=src, d=d):
-                remote(landed, landed, z_s.at[idx, d - 1], z_r.at[idx, d - 1], h, src).wait_recv()
-            when(used, wait)
-            start(both(used, q != src),
-                  remote(landed, sig.at[idx, :, chip_cols(q)], fwd_s.at[idx, d - 1], sig_r.at[idx, q],
-                         src * CORES + c, s))
-
-            def keep(d=d):
-                sig[idx, :, chip_cols(q)] = relay[idx, d - 1]
-            when(both(used, q == src), keep)
+            remote(landed, landed, z_s.at[idx, d - 1], z_r.at[idx, d - 1], h, lax.rem(s + planes - 1, planes)).wait_recv()
+        when(used, wait)
+        if d < planes - 1:
+            start(both(used, s + 1 < planes), up_copy(idx, d))
+        pass_on(idx, d - 1, s - d, used)
+
+    def stage_down(b, i):
+        idx = b * steps + i
+        for e in range(1, below + 1):
+            used = both(mine, s + e < planes, live((s + e) * CORES + c, s))
+            when(used, down_copy(idx, e, s + e).wait_recv)
+            pass_on(idx, planes - 2 + e, s + e, used)
+
+    def forward_first(b, i):
+        stage_up(b, i, 1)
+
+    def forward_rest(b, i):
+        for d in range(2, planes):
+            stage_up(b, i, d)
+        stage_down(b, i)
 
     def stage_gather(i):
         rows = slice(i * row_t, (i + 1) * row_t)
@@ -241,30 +283,43 @@
                 remote(spot, spot, mg_s.at[i, d], mg_r.at[i, d], mate, s).wait_recv()
             when(owns(src), wait)
 
-    make_mask(0)
-    for b in range(blocks):
+    load_first.wait()
+    load_self.wait()
+    make_mask(0, 1 - c)
+    load_second.wait()
+    make_mask(0, c)
+    for i in range(steps):
+        stage_product(0, i)
+    for i in range(steps):
+        stage_pair(0, i)
+    for load in load_small:
+        load.wait()
+    row = lax.broadcasted_iota(jnp.int32, (row_t, row_t), 0)
+    col = lax.broadcasted_iota(jnp.int32, (row_t, row_t), 1)
+    spread = jnp.where(row == col, jnp.broadcast_to(coup_ref[...], (row_t, row_t)), 0.0)
+    weights[...] = jnp.broadcast_to(jnp.sum(spread, axis=1, keepdims=True), weights.shape)
+
+    def first_green():
+        green[...] = edge_ref[:, chip_cols(q)].astype(F32)
+    when(mine, first_green)
+    for i in range(steps):
+        stage_reduce(0, i)
+    for b in range(1, blocks):
+        make_mask(b, 0)
+        make_mask(b, 1)
+        forward_first(b - 1, 0)
+        forward_rest(b - 1, 0)
         for i in range(steps):
+            if i + 1 < steps:
+                forward_first(b - 1, i + 1)
             stage_product(b, i)
-        for i in range(steps):
             stage_pair(b, i)
-        if b == 0:
-            row = lax.broadcasted_iota(jnp.int32, (row_t, row_t), 0)
-            col = lax.broadcasted_iota(jnp.int32, (row_t, row_t), 1)
-            spread = jnp.where(row == col, jnp.broadcast_to(coup_ref[...], (row_t, row_t)), 0.0)
-            weights[...] = jnp.broadcast_to(jnp.sum(spread, axis=1, keepdims=True), weights.shape)
-
-            def first_green():
-                green[...] = edge_ref[:, own_cols(q, c)].astype(F32)
-            when(mine, first_green)
-        if b + 1 < blocks:
-            make_mask(b + 1)
-        for i in range(steps):
+            if i + 1 < steps:
+                forward_rest(b - 1, i + 1)
+            if b + 1 == blocks and i:
+                stage_gather(i - 1)
             stage_reduce(b, i)
-        for i in range(steps):
-            if b + 1 < blocks:
-                stage_forward(b, i)
-            else:
-                stage_gather(i)
+    stage_gather(steps - 1)
     for i in range(steps):
         stage_close(i)
     for cond, copy in pending:
@@ -281,16 +336,25 @@
     owners = min(chips, half // LANES)
     width = half // owners
     assert chips == planes and half == slab
-    dims = (chips, planes, owners, width, row_t, steps, blocks)
+    past, tiles = slab // row_t, cols // row_t
+    below = (tiles + 2 + 2 * (blocks - 1)) // (CORES * past)
+    slots = planes - 1 + below
+    dims = (chips, planes, owners, width, row_t, steps, blocks, below)
     n, m = blocks * steps, (blocks - 1) * steps
     vmem = pl.BlockSpec(memory_space=pltpu.VMEM)
     dma = pltpu.SemaphoreType.DMA
     return pl.pallas_call(
         functools.partial(kernel, dims),
         out_shape=jax.ShapeDtypeStruct((steps * row_t, cols), BF16),
-        in_specs=[vmem] * 5 + [pl.BlockSpec(memory_space=pltpu.SMEM)],
+        in_specs=[pl.BlockSpec(memory_space=pl.ANY)] * 5 + [pl.BlockSpec(memory_space=pltpu.SMEM)],
         out_specs=vmem,
         scratch_shapes=[
+            pltpu.VMEM((slab, cols), BF16),
+            pltpu.VMEM(self_rows.shape, BF16),
+            pltpu.VMEM((row_t, half), BF16),
+            pltpu.VMEM((row_t, row_t), F32),
+            pltpu.VMEM((1, row_t), F32),
+            dma((6,)),
             pltpu.VMEM((blocks, slab, cols), BF16),
             pltpu.VMEM((n, row_t, half), BF16),
             pltpu.VMEM((n, row_t, half), BF16),
@@ -301,17 +365,17 @@
             pltpu.VMEM((row_t, width), F32),
             pltpu.VMEM((row_t, width), F32),
             pltpu.VMEM((m, row_t, width), BF16),
-            pltpu.VMEM((m, planes - 1, row_t, width), BF16),
+            pltpu.VMEM((m, slots, row_t, width), BF16),
             pltpu.VMEM((m, row_t, slab), BF16),
             dma((n,)), dma((n,)),
             dma((n, chips - 1)), dma((n, chips - 1)),
-            dma((m, planes - 1)), dma((m, planes - 1)),
-            dma((m,)), dma((m, planes - 1)), dma((m, chips)),
+            dma((m, slots)), dma((m, slots)),
+            dma((m,)), dma((m, slots)), dma((m, chips)),
             dma((steps, chips - 1)), dma((steps, chips - 1)),
             dma((steps, chips)), dma((steps, chips)),
         ],
         compiler_params=pltpu.CompilerParams(
-            collective_id=0, has_side_effects=True, vmem_limit_bytes=48 * 1024 * 1024),
+            collective_id=0, has_side_effects=True, vmem_limit_bytes=56 * 1024 * 1024),
         cost_estimate=pl.CostEstimate(
             flops=2 * blocks * steps * row_t * slab * cols, bytes_accessed=2 * slab * cols, transcendentals=0),
     )(history, self_rows, edge_rows, step_inv, coupling.reshape(1, row_t), reach)

time: 72.2 us -> 80.3 us (1.11)
  Pallas kernels: 66.6 us -> 77.8 us
  local copies, waits for them, and re-layouts: 5.23 us -> 2.3 us
    pallas_call x1, Pallas kernels: 66.6 us -> 77.8 us  [local(): pl.pallas_call(functools.partial(kernel, dims), out_shape=jax.ShapeDtypeS...]
    unnamed x11 -> x1, local copies, waits for them, and re-layouts: 5.23 us -> 2.3 us
where the time goes in v2:
time: 80.3 us; the launch traced here: 80.1 us
  Pallas kernels  77.8 us (97%)
  local copies, waits for them, and re-layouts  2.3 us (3%)
    pallas_call x1, Pallas kernels, local(): pl.pallas_call(functools.partial(kernel, dims), out_shape=jax.ShapeDtypeS...  77.8 us
    unnamed x1, local copies, waits for them, and re-layouts  2.3 us

profile of v2, /device:TPU:25, one launch (start us, length us, event | category | flops | bytes accessed | tf_op | source)
XLA Modules:
  0.0 80.1 jit_solution(11741219330549437777)
XLA Ops:
  0.0 77.8 %shard_map.64 = bf16[256,2048]{1,0:T(8,128)(2,1)} custom-call(bf16[1024,2048]{1,0:T(8,128)(2,1)} %hist_hbm.1, bf16[256,1024]{1,0:T(8,128)(2,1)} %self_hbm.1, bf16[128,2048]{1,0:T(8,128)(2,1)} %edge_hbm.1, f32[128,128]{1,0:T(8,128)} %inv_hbm.1, f32[1,128]{1,0:T(1,128)} %bitcast.1, s32[3,64]{1,0:T(4,128)} %reach_ref.1), custom_call_target="tpu_custom_call" | custom-call | flops 3221225472 | bytes 4194304 | tf_op jit(solution)/shard_map/pallas_call | solution.py:346
  77.8 2.3 %copy.8 = bf16[256,2048]{1,0:T(8,128)(2,1)} copy(bf16[256,2048]{1,0:T(8,128)(2,1)} %shard_map.64) | data formatting | bytes 2097152

commit v3 on v1

--- a/solution.py
+++ b/solution.py
@@ -202,9 +202,9 @@
             sig[idx, :, chip_cols(q)] = piece[idx]
         when(both(mine, q == s), keep)
 
-    def stage_forward(b, i):
-        idx = b * steps + i
-        for d in range(1, planes):
+    def stage_forward(b, i, first, stop):
+        idx = b * steps + i
+        for d in range(first, stop):
             src = lax.rem(s + planes - d, planes)
             used = both(mine, live(src * CORES + c, s))
             landed = relay.at[idx, d - 1]
@@ -242,29 +242,35 @@
             when(owns(src), wait)
 
     make_mask(0)
-    for b in range(blocks):
+    for i in range(steps):
+        stage_product(0, i)
+    for i in range(steps):
+        stage_pair(0, i)
+    row = lax.broadcasted_iota(jnp.int32, (row_t, row_t), 0)
+    col = lax.broadcasted_iota(jnp.int32, (row_t, row_t), 1)
+    spread = jnp.where(row == col, jnp.broadcast_to(coup_ref[...], (row_t, row_t)), 0.0)
+    weights[...] = jnp.broadcast_to(jnp.sum(spread, axis=1, keepdims=True), weights.shape)
+
+    def first_green():
+        green[...] = edge_ref[:, own_cols(q, c)].astype(F32)
+    when(mine, first_green)
+    for b in range(1, blocks):
         for i in range(steps):
+            stage_reduce(b - 1, i)
+        make_mask(b)
+        stage_forward(b - 1, 0, 1, planes)
+        if steps > 1:
+            stage_forward(b - 1, 1, 1, 2)
+        stage_product(b, 0)
+        stage_pair(b, 0)
+        for i in range(1, steps):
+            stage_forward(b - 1, i, 2 if i == 1 else 1, planes)
             stage_product(b, i)
-        for i in range(steps):
             stage_pair(b, i)
-        if b == 0:
-            row = lax.broadcasted_iota(jnp.int32, (row_t, row_t), 0)
-            col = lax.broadcasted_iota(jnp.int32, (row_t, row_t), 1)
-            spread = jnp.where(row == col, jnp.broadcast_to(coup_ref[...], (row_t, row_t)), 0.0)
-            weights[...] = jnp.broadcast_to(jnp.sum(spread, axis=1, keepdims=True), weights.shape)
-
-            def first_green():
-                green[...] = edge_ref[:, own_cols(q, c)].astype(F32)
-            when(mine, first_green)
-        if b + 1 < blocks:
-            make_mask(b + 1)
-        for i in range(steps):
-            stage_reduce(b, i)
-        for i in range(steps):
-            if b + 1 < blocks:
-                stage_forward(b, i)
-            else:
-                stage_gather(i)
+    for i in range(steps):
+        stage_reduce(blocks - 1, i)
+    for i in range(steps):
+        stage_gather(i)
     for i in range(steps):
         stage_close(i)
     for cond, copy in pending:

time: 72.2 us -> 83.5 us (1.16)
  the two profiles are of different devices: /device:TPU:25 before, /device:TPU:17 now
where the time goes in v3:
time: 83.5 us; the launch traced here: 83.1 us
  Pallas kernels  77.9 us (93%)
  local copies, waits for them, and re-layouts  5.23 us (6%)
    pallas_call x1, Pallas kernels, local(): pl.pallas_call(functools.partial(kernel, dims), out_shape=jax.ShapeDtypeS...  77.9 us
    unnamed x11, local copies, waits for them, and re-layouts  5.23 us

profile of v3, /device:TPU:17, one launch (start us, length us, event | category | flops | bytes accessed | tf_op | source)
XLA Modules:
  0.0 83.1 jit_solution(17445706967228366462)
XLA Ops:
  0.0 0.0 copy-start
  0.0 1.0 %copy-done = bf16[256,1024]{1,0:T(8,128)(2,1)S(1)} copy-done((bf16[256,1024]{1,0:T(8,128)(2,1)S(1)}, bf16[256,1024]{1,0:T(8,128)(2,1)}, u32[]{:S(2)}) %copy-start) | copy-done | bytes 524312
  1.0 0.0 copy-start.1
  1.0 1.0 %copy-done.1 = bf16[128,2048]{1,0:T(8,128)(2,1)S(1)} copy-done((bf16[128,2048]{1,0:T(8,128)(2,1)S(1)}, bf16[128,2048]{1,0:T(8,128)(2,1)}, u32[]{:S(2)}) %copy-start.1) | copy-done | bytes 524312
  2.1 0.0 copy-start.2
  2.1 0.8 %copy-done.2 = f32[128,128]{1,0:T(8,128)S(1)} copy-done((f32[128,128]{1,0:T(8,128)S(1)}, f32[128,128]{1,0:T(8,128)}, u32[]{:S(2)}) %copy-start.2) | copy-done | bytes 65560
  2.9 0.0 copy-start.3
  2.9 0.7 copy-done.3
  3.6 0.0 copy-start.4
  3.6 0.7 copy-done.4
  4.3 77.9 %shard_map.64 = bf16[256,2048]{1,0:T(8,128)(2,1)S(1)} custom-call(bf16[1024,2048]{1,0:T(8,128)(2,1)} %hist_ref.1, bf16[256,1024]{1,0:T(8,128)(2,1)S(1)} %copy-done, bf16[128,2048]{1,0:T(8,128)(2,1)S(1)} %copy-done.1, f32[128,128]{1,0:T(8,128)S(1)} %copy-done.2, f32[1,128]{1,0:T(1,128)S(1)} %bitcast.1, s32[3,64]{1,0:T(4,128)S(1)} %copy-done.3), custom_call_target="tpu_custom_call" | custom-call | flops 3221225472 | bytes 4194304 | tf_op jit(solution)/shard_map/pallas_call | solution.py:294
  82.2 1.0 %copy.8 = bf16[256,2048]{1,0:T(8,128)(2,1)} copy(bf16[256,2048]{1,0:T(8,128)(2,1)S(1)} %shard_map.64) | data formatting | bytes 2097152
Async XLA Ops:
  0.0 1.0 %copy-start = (bf16[256,1024]{1,0:T(8,128)(2,1)S(1)}, bf16[256,1024]{1,0:T(8,128)(2,1)}, u32[]{:S(2)}) copy-start(bf16[256,1024]{1,0:T(8,128)(2,1)} %self_ref.1) | copy-start | bytes 1572868
  1.0 1.0 %copy-start.1 = (bf16[128,2048]{1,0:T(8,128)(2,1)S(1)}, bf16[128,2048]{1,0:T(8,128)(2,1)}, u32[]{:S(2)}) copy-start(bf16[128,2048]{1,0:T(8,128)(2,1)} %edge_ref.1) | copy-start | bytes 1572868
  2.1 0.8 %copy-start.2 = (f32[128,128]{1,0:T(8,128)S(1)}, f32[128,128]{1,0:T(8,128)}, u32[]{:S(2)}) copy-start(f32[128,128]{1,0:T(8,128)} %inv_ref.1) | copy-start | bytes 196612
  2.9 0.7 copy-start.3
  3.6 0.7 copy-start.4

commit v4 on v2

--- a/solution.py
+++ b/solution.py
@@ -288,38 +288,33 @@
     make_mask(0, 1 - c)
     load_second.wait()
     make_mask(0, c)
-    for i in range(steps):
-        stage_product(0, i)
-    for i in range(steps):
-        stage_pair(0, i)
-    for load in load_small:
-        load.wait()
-    row = lax.broadcasted_iota(jnp.int32, (row_t, row_t), 0)
-    col = lax.broadcasted_iota(jnp.int32, (row_t, row_t), 1)
-    spread = jnp.where(row == col, jnp.broadcast_to(coup_ref[...], (row_t, row_t)), 0.0)
-    weights[...] = jnp.broadcast_to(jnp.sum(spread, axis=1, keepdims=True), weights.shape)
-
-    def first_green():
-        green[...] = edge_ref[:, chip_cols(q)].astype(F32)
-    when(mine, first_green)
-    for i in range(steps):
-        stage_reduce(0, i)
-    for b in range(1, blocks):
-        make_mask(b, 0)
-        make_mask(b, 1)
-        forward_first(b - 1, 0)
-        forward_rest(b - 1, 0)
+    for b in range(blocks):
         for i in range(steps):
-            if i + 1 < steps:
-                forward_first(b - 1, i + 1)
             stage_product(b, i)
+        for i in range(steps):
             stage_pair(b, i)
-            if i + 1 < steps:
-                forward_rest(b - 1, i + 1)
-            if b + 1 == blocks and i:
-                stage_gather(i - 1)
+        if b == 0:
+            for load in load_small:
+                load.wait()
+            row = lax.broadcasted_iota(jnp.int32, (row_t, row_t), 0)
+            col = lax.broadcasted_iota(jnp.int32, (row_t, row_t), 1)
+            spread = jnp.where(row == col, jnp.broadcast_to(coup_ref[...], (row_t, row_t)), 0.0)
+            weights[...] = jnp.broadcast_to(jnp.sum(spread, axis=1, keepdims=True), weights.shape)
+
+            def first_green():
+                green[...] = edge_ref[:, chip_cols(q)].astype(F32)
+            when(mine, first_green)
+        if b + 1 < blocks:
+            make_mask(b + 1, 0)
+            make_mask(b + 1, 1)
+        for i in range(steps):
             stage_reduce(b, i)
-    stage_gather(steps - 1)
+        for i in range(steps):
+            if b + 1 < blocks:
+                forward_first(b, i)
+                forward_rest(b, i)
+            else:
+                stage_gather(i)
     for i in range(steps):
         stage_close(i)
     for cond, copy in pending:

time: 80.3 us -> 70.5 us (0.88)
  Pallas kernels: 77.8 us -> 68 us
    pallas_call x1, Pallas kernels: 77.8 us -> 68 us  [local(): pl.pallas_call(functools.partial(kernel, dims), out_shape=jax.ShapeDtypeS...]
where the time goes in v4:
time: 70.5 us; the launch traced here: 70.3 us
  Pallas kernels  68 us (96%)
  local copies, waits for them, and re-layouts  2.3 us (3%)
    pallas_call x1, Pallas kernels, local(): pl.pallas_call(functools.partial(kernel, dims), out_shape=jax.ShapeDtypeS...  68 us
    unnamed x1, local copies, waits for them, and re-layouts  2.3 us

profile of v4, /device:TPU:25, one launch (start us, length us, event | category | flops | bytes accessed | tf_op | source)
XLA Modules:
  0.0 70.3 jit_solution(10789492022578773747)
XLA Ops:
  0.0 68.0 %shard_map.64 = bf16[256,2048]{1,0:T(8,128)(2,1)} custom-call(bf16[1024,2048]{1,0:T(8,128)(2,1)} %hist_hbm.1, bf16[256,1024]{1,0:T(8,128)(2,1)} %self_hbm.1, bf16[128,2048]{1,0:T(8,128)(2,1)} %edge_hbm.1, f32[128,128]{1,0:T(8,128)} %inv_hbm.1, f32[1,128]{1,0:T(1,128)} %bitcast.1, s32[3,64]{1,0:T(4,128)} %reach_ref.1), custom_call_target="tpu_custom_call" | custom-call | flops 3221225472 | bytes 4194304 | tf_op jit(solution)/shard_map/pallas_call | solution.py:341
  68.0 2.3 %copy.8 = bf16[256,2048]{1,0:T(8,128)(2,1)} copy(bf16[256,2048]{1,0:T(8,128)(2,1)} %shard_map.64) | data formatting | bytes 2097152

commit v5 on v4

--- a/solution.py
+++ b/solution.py
@@ -106,15 +106,17 @@
             lax.fori_loop(0, tiles // CORES, body, 0)
         when(live_me, work)
 
-    def product(b, i, dst, core):
-        idx = b * steps + i
+    def product(b, dst, core):
+        base = b * steps
         chunk = 256
 
         def body(t, carry):
-            left = self_ref[i * row_t:(i + 1) * row_t, :] if b == 0 else sig[idx - steps]
+            left = self_ref[...] if b == 0 else sig[base - steps:base].reshape(steps * row_t, slab)
             at = pl.ds(pl.multiple_of(core * half + t * chunk, chunk), chunk)
             to = pl.ds(pl.multiple_of(t * chunk, chunk), chunk)
-            dst[idx, :, to] = jnp.dot(left, masked[b, :, at], preferred_element_type=F32).astype(BF16)
+            result = jnp.dot(left, masked[b, :, at], preferred_element_type=F32).astype(BF16)
+            for i in range(steps):
+                dst[base + i, :, to] = result[i * row_t:(i + 1) * row_t]
             return carry
         lax.fori_loop(0, half // chunk, body, 0)
 
@@ -130,18 +132,23 @@
                 remote(spot, spot, home_s.at[idx], sig_r.at[idx, p], p * CORES + c, s).wait_recv()
             when(owns(p), wait)
 
-    def stage_product(b, i):
-        idx = b * steps + i
+    def stage_product(b):
+        base = b * steps
 
         def first():
             if b:
-                sig_wait(idx - steps)
-            product(b, i, psend, 1 - c)
+                for i in range(steps):
+                    sig_wait(base - steps + i)
+            product(b, psend, 1 - c)
         when(live_me, first)
-        if idx == 0:
+        if b == 0:
             pl.semaphore_wait(barrier, 1 + (chips - 1) + (planes - 1))
-        start(live_me, a0_copy(idx))
-        when(live_me, lambda: product(b, i, pown, c))
+        for i in range(steps):
+            start(live_me, a0_copy(base + i))
+        if b == 0:
+            load_second.wait()
+            make_mask(0, c)
+        when(live_me, lambda: product(b, pown, c))
 
     def a1_copy(idx, d):
         to = lax.rem(q + d, chips)
@@ -286,11 +293,8 @@
     load_first.wait()
     load_self.wait()
     make_mask(0, 1 - c)
-    load_second.wait()
-    make_mask(0, c)
     for b in range(blocks):
-        for i in range(steps):
-            stage_product(b, i)
+        stage_product(b)
         for i in range(steps):
             stage_pair(b, i)
         if b == 0:

time: 70.5 us -> 70.5 us (level)
  no operation moved by 1% of the time
where the time goes in v5:
time: 70.5 us; the launch traced here: 70.4 us
  Pallas kernels  68 us (96%)
  local copies, waits for them, and re-layouts  2.3 us (3%)
    pallas_call x1, Pallas kernels, local(): pl.pallas_call(functools.partial(kernel, dims), out_shape=jax.ShapeDtypeS...  68 us
    unnamed x1, local copies, waits for them, and re-layouts  2.3 us

profile of v5, /device:TPU:25, one launch (start us, length us, event | category | flops | bytes accessed | tf_op | source)
XLA Modules:
  0.0 70.4 jit_solution(3367122141877222095)
XLA Ops:
  0.0 68.0 %shard_map.64 = bf16[256,2048]{1,0:T(8,128)(2,1)} custom-call(bf16[1024,2048]{1,0:T(8,128)(2,1)} %hist_hbm.1, bf16[256,1024]{1,0:T(8,128)(2,1)} %self_hbm.1, bf16[128,2048]{1,0:T(8,128)(2,1)} %edge_hbm.1, f32[128,128]{1,0:T(8,128)} %inv_hbm.1, f32[1,128]{1,0:T(1,128)} %bitcast.1, s32[3,64]{1,0:T(4,128)} %reach_ref.1), custom_call_target="tpu_custom_call" | custom-call | flops 3221225472 | bytes 4194304 | tf_op jit(solution)/shard_map/pallas_call | solution.py:345
  68.1 2.3 %copy.8 = bf16[256,2048]{1,0:T(8,128)(2,1)} copy(bf16[256,2048]{1,0:T(8,128)(2,1)} %shard_map.64) | data formatting | bytes 2097152

commit v6 on v5

--- a/solution.py
+++ b/solution.py
@@ -261,14 +261,6 @@
             when(used, down_copy(idx, e, s + e).wait_recv)
             pass_on(idx, planes - 2 + e, s + e, used)
 
-    def forward_first(b, i):
-        stage_up(b, i, 1)
-
-    def forward_rest(b, i):
-        for d in range(2, planes):
-            stage_up(b, i, d)
-        stage_down(b, i)
-
     def stage_gather(i):
         rows = slice(i * row_t, (i + 1) * row_t)
         for d in range(1, chips):
@@ -313,11 +305,14 @@
             make_mask(b + 1, 1)
         for i in range(steps):
             stage_reduce(b, i)
-        for i in range(steps):
-            if b + 1 < blocks:
-                forward_first(b, i)
-                forward_rest(b, i)
-            else:
+        if b + 1 < blocks:
+            for d in range(1, planes):
+                for i in range(steps):
+                    stage_up(b, i, d)
+            for i in range(steps):
+                stage_down(b, i)
+        else:
+            for i in range(steps):
                 stage_gather(i)
     for i in range(steps):
         stage_close(i)

time: 70.5 us -> 72.8 us (1.033)
  Pallas kernels: 68 us -> 70.3 us
    pallas_call x1, Pallas kernels: 68 us -> 70.3 us  [local(): pl.pallas_call(functools.partial(kernel, dims), out_shape=jax.ShapeDtypeS...]
where the time goes in v6:
time: 72.8 us; the launch traced here: 72.6 us
  Pallas kernels  70.3 us (97%)
  local copies, waits for them, and re-layouts  2.3 us (3%)
    pallas_call x1, Pallas kernels, local(): pl.pallas_call(functools.partial(kernel, dims), out_shape=jax.ShapeDtypeS...  70.3 us
    unnamed x1, local copies, waits for them, and re-layouts  2.3 us

profile of v6, /device:TPU:25, one launch (start us, length us, event | category | flops | bytes accessed | tf_op | source)
XLA Modules:
  0.0 72.6 jit_solution(4586501116572875574)
XLA Ops:
  0.0 70.3 %shard_map.64 = bf16[256,2048]{1,0:T(8,128)(2,1)} custom-call(bf16[1024,2048]{1,0:T(8,128)(2,1)} %hist_hbm.1, bf16[256,1024]{1,0:T(8,128)(2,1)} %self_hbm.1, bf16[128,2048]{1,0:T(8,128)(2,1)} %edge_hbm.1, f32[128,128]{1,0:T(8,128)} %inv_hbm.1, f32[1,128]{1,0:T(1,128)} %bitcast.1, s32[3,64]{1,0:T(4,128)} %reach_ref.1), custom_call_target="tpu_custom_call" | custom-call | flops 3221225472 | bytes 4194304 | tf_op jit(solution)/shard_map/pallas_call | solution.py:340
  70.3 2.3 %copy.8 = bf16[256,2048]{1,0:T(8,128)(2,1)} copy(bf16[256,2048]{1,0:T(8,128)(2,1)} %shard_map.64) | data formatting | bytes 2097152

commit v7 on v4

--- a/solution.py
+++ b/solution.py
@@ -370,7 +370,7 @@
             dma((steps, chips)), dma((steps, chips)),
         ],
         compiler_params=pltpu.CompilerParams(
-            collective_id=0, has_side_effects=True, vmem_limit_bytes=56 * 1024 * 1024),
+            collective_id=0, has_side_effects=True, vmem_limit_bytes=54 * 1024 * 1024),
         cost_estimate=pl.CostEstimate(
             flops=2 * blocks * steps * row_t * slab * cols, bytes_accessed=2 * slab * cols, transcendentals=0),
     )(history, self_rows, edge_rows, step_inv, coupling.reshape(1, row_t), reach)

time: 70.5 us -> 70.5 us (level)
  no operation moved by 1% of the time
where the time goes in v7:
time: 70.5 us; the launch traced here: 70.3 us
  Pallas kernels  68 us (96%)
  local copies, waits for them, and re-layouts  2.3 us (3%)
    pallas_call x1, Pallas kernels, local(): pl.pallas_call(functools.partial(kernel, dims), out_shape=jax.ShapeDtypeS...  68 us
    unnamed x1, local copies, waits for them, and re-layouts  2.3 us

profile of v7, /device:TPU:25, one launch (start us, length us, event | category | flops | bytes accessed | tf_op | source)
XLA Modules:
  0.0 70.3 jit_solution(10789492022578773747)
XLA Ops:
  0.0 68.0 %shard_map.64 = bf16[256,2048]{1,0:T(8,128)(2,1)} custom-call(bf16[1024,2048]{1,0:T(8,128)(2,1)} %hist_hbm.1, bf16[256,1024]{1,0:T(8,128)(2,1)} %self_hbm.1, bf16[128,2048]{1,0:T(8,128)(2,1)} %edge_hbm.1, f32[128,128]{1,0:T(8,128)} %inv_hbm.1, f32[1,128]{1,0:T(1,128)} %bitcast.1, s32[3,64]{1,0:T(4,128)} %reach_ref.1), custom_call_target="tpu_custom_call" | custom-call | flops 3221225472 | bytes 4194304 | tf_op jit(solution)/shard_map/pallas_call | solution.py:341
  68.0 2.3 %copy.8 = bf16[256,2048]{1,0:T(8,128)(2,1)} copy(bf16[256,2048]{1,0:T(8,128)(2,1)} %shard_map.64) | data formatting | bytes 2097152
